TPU v7x, 128 devices: a whole 4x4x4 slice. The times are simulated.
128 devices in a mesh: row: 32 (over y, z, core), col: 4 (over x).
Axes of the slice: x: 4, y: 4, z: 4, core: 2. Of those that a mesh axis runs over, the one named last changes fastest.
Arguments:
- tile_values: bfloat16 [5632, 4, 256, 256], P('row', 'col'), may hold values from -0.375 to 0.375
- tile_rows: int32 [5632, 4], P('row', 'col'), may hold values from 0 to 15, as said below
- tile_source: int32 [5632, 4], P('row', 'col'), may hold values from 0 to 31
- tile_slot: int32 [5632, 4], P('row', 'col'), may hold values from 0 to 1
- send_lists: int32 [32, 4, 32, 2], P('row', 'col'), may hold values from 0 to 7
- basis_blocks: bfloat16 [256, 4, 256, 256], P('row', 'col'), may hold values from -6 to 6
Outputs:
- new_basis: float32 [131072, 256], P(('row', 'col'))
- triangle: float32 [256, 256], replicated
Inputs may be any that keep to these rules, and one draw needn't show every extreme that they name: `tile_rows`: in every slab and group each of the 16 block rows holds at least one tile.
All inputs are finite; a program needn't handle non-finite values.
Results may differ from a plain program's by a relative error of at most 0.0015.
Values may be sent and summed in bfloat16 or wider, within the bound.
No kernel may reach another device: no remote copies, remote signals or barrier semaphores. Data moves between devices by JAX's collectives and lax.ppermute only.
A program may use at most 256 MiB of HBM per device.

v0:
```python
import jax
import jax.numpy as jnp
from jax import lax
from jax.sharding import PartitionSpec as P

BR_DEV = 16


def upper_factor(gram):
    width = gram.shape[0]
    index = jnp.arange(width, dtype=jnp.int32)

    def row_fill(j, upper):
        unit = (index == j).astype(jnp.float32)
        known = jnp.dot(upper, unit, precision=lax.Precision.HIGHEST)
        target = lax.dynamic_index_in_dim(gram, j, 0, keepdims=False)
        residue = target - jnp.dot(known, upper, precision=lax.Precision.HIGHEST)
        pivot = jnp.sqrt(lax.dynamic_index_in_dim(residue, j, 0, keepdims=False))
        filled = jnp.where(index >= j, residue / pivot, jnp.float32(0.0))
        return upper + unit[:, None] * filled[None, :]

    return lax.fori_loop(0, width, row_fill, jnp.zeros((width, width), jnp.float32))


def upper_inverse(upper):
    width = upper.shape[0]
    index = jnp.arange(width, dtype=jnp.int32)

    def row_step(step, inverse):
        i = (width - 1 - step).astype(jnp.int32)
        row_now = lax.dynamic_index_in_dim(upper, i, 0, keepdims=False)
        pivot = lax.dynamic_index_in_dim(row_now, i, 0, keepdims=False)
        unit = (index == i).astype(jnp.float32)
        solved = (unit - jnp.dot(row_now, inverse, precision=lax.Precision.HIGHEST)) / pivot
        return jnp.where((index == i)[:, None], solved[None, :], inverse)

    return lax.fori_loop(0, width, row_step, jnp.zeros((width, width), jnp.float32))


def local(tile_values, tile_rows, tile_source, tile_slot, send_lists, basis_blocks):
    values = tile_values[:, 0]
    blocks_row = tile_rows[:, 0]
    source = tile_source[:, 0]
    slotted = tile_slot[:, 0]
    owned = basis_blocks[:, 0]
    slot_count = send_lists.shape[3]
    rank_width = owned.shape[2]
    outgoing = owned[send_lists[0, 0]]
    arrived = lax.all_to_all(outgoing, "row", split_axis=0, concat_axis=0, tiled=True)
    flatten = arrived.reshape(-1, arrived.shape[2], arrived.shape[3])
    chosen = flatten[source * slot_count + slotted]
    product = jnp.einsum("tij,tjk->tik", values, chosen, preferred_element_type=jnp.float32)
    selector = (blocks_row[None, :] == jnp.arange(BR_DEV, dtype=jnp.int32)[:, None]).astype(
        jnp.float32
    )
    partial_value = jnp.einsum("bt,tik->bik", selector, product, precision=lax.Precision.HIGHEST)
    partial_value = partial_value.reshape(-1, rank_width)
    local_y = lax.psum_scatter(partial_value, "col", scatter_dimension=0, tiled=True)
    gram = jnp.dot(local_y.T, local_y, precision=lax.Precision.HIGHEST)
    summed = lax.psum(gram, ("row", "col"))
    upper = upper_factor(summed)
    cells_all = local_y.shape[0] * lax.axis_size("row") * lax.axis_size("col")
    scale = jnp.sqrt(jnp.float32(cells_all))
    solved = jnp.dot(local_y, upper_inverse(upper), precision=lax.Precision.HIGHEST)
    return (solved * scale, upper / scale)


def solution(mesh):
    return jax.shard_map(
        local,
        mesh=mesh,
        in_specs=(
            P("row", "col", None, None),
            P("row", "col"),
            P("row", "col"),
            P("row", "col"),
            P("row", "col", None, None),
            P("row", "col", None, None),
        ),
        out_specs=(P(("row", "col"), None), P()),
        check_vma=False,
    )
```

profile of v0, /device:TPU:1, one launch (start us, length us, event | category | flops | bytes accessed | tf_op | source)
XLA Modules:
  0.0 1576.3 jit_solution(10319401639767442812)
XLA Ops:
  7.2 0.8 compare_select_fusion.2
  8.4 5.5 gather_fusion
  13.9 9.6 all-to-all-start
  23.7 108.4 %all-to-all-done = bf16[32,2,256,256]{3,2,1,0:T(8,128)(2,1)} async-done(((bf16[32,2,256,256]{3,2,1,0:T(8,128)(2,1)}), bf16[32,2,256,256]{3,2,1,0:T(8,128)(2,1)}, u32[]{:S(2)}, u32[]{:S(2)}) %all-to-all-start) | async-done | bytes 8388640 | tf_op jit(solution)/shard_map/all_to_all | solution.py:49
  132.1 13.8 gather_fusion.1
  145.9 37.6 %fusion.24 = f32[176,256,256]{2,1,0:T(8,128)} fusion(bf16[176,256,256]{2,1,0:T(8,128)(2,1)} %gather_fusion.1, bf16[176,1,256,256]{3,2,1,0:T(8,128)(2,1)} %param.10), kind=kOutput, calls=%fused_computation.32 | convolution fusion | flops 5905580032 | bytes 92274688 | tf_op jit(solution)/shard_map/tij,tjk->tik/dot_general | solution.py:52
  183.5 46.6 %copy.11 = f32[176,256,256]{1,0,2:T(8,128)} copy(f32[176,256,256]{2,1,0:T(8,128)} %fusion.24) | data formatting | bytes 92274688 | tf_op jit(solution)/shard_map/tij,tjk->tik/dot_general | solution.py:52
  230.1 20.4 %fusion.22 = f32[16,256,256]{2,0,1:T(8,128)S(1)} fusion(f32[176,256,256]{1,0,2:T(8,128)} %copy.11, s32[176]{0:T(256)S(1)} %bitcast.63), kind=kOutput, calls=%fused_computation.30 | convolution fusion | flops 2214595328 | bytes 50332352 | tf_op jit(solution)/shard_map/bt,tik->bik/dot_general | solution.py:56
  250.5 4.4 copy.10
  255.1 61.9 %reduce-scatter.2.cloned.1.call-done = f32[1024,256]{1,0:T(8,128)} async-done(((f32[4096,256]{1,0:T(8,128)}), f32[1024,256]{1,0:T(8,128)}) %reduce-scatter.2.cloned.1.call-update) | async-done | bytes 1048592 | tf_op jit(solution)/shard_map/reduce_scatter | solution.py:58
  317.0 4.1 fusion.29
  321.1 143.2 %all-reduce.2.cloned.1.call-done = f32[256,256]{1,0:T(8,128)} async-done(((f32[256,256]{1,0:T(8,128)}), f32[256,256]{1,0:T(8,128)}) %all-reduce.2.cloned.1.call-update) | async-done | bytes 262160 | tf_op jit(solution)/shard_map/psum | solution.py:60
  464.3 680.8 %while.33 = (s32[]{:T(128)}, f32[256,256]{1,0:T(8,128)S(1)}, f32[256,256]{1,0:T(8,128)}, s32[]{:T(128)}, s32[]{:T(128)}) while((s32[]{:T(128)}, f32[256,256]{1,0:T(8,128)S(1)}, f32[256,256]{1,0:T(8,128)}, s32[]{:T(128)}, s32[]{:T(128)}) %tuple.80), condition=%wide.region_3.4_spmd.clone.clone, body=%wide.region_2.3_spmd.clone.clone.sunk | while | flops 1902083 | bytes 1063021 | solution.py:22
  467.5 0.7 constant_dynamic-slice_fusion.2
  470.1 0.7 constant_dynamic-slice_fusion.2
  475.4 0.7 constant_dynamic-slice_fusion.2
  478.1 0.7 constant_dynamic-slice_fusion.2
  486.1 0.7 constant_dynamic-slice_fusion.2
  494.1 0.7 constant_dynamic-slice_fusion.2
  496.7 0.7 constant_dynamic-slice_fusion.2
  502.0 0.7 constant_dynamic-slice_fusion.2
  504.7 0.7 constant_dynamic-slice_fusion.2
  510.0 0.7 constant_dynamic-slice_fusion.2
  512.7 0.7 constant_dynamic-slice_fusion.2
  518.0 0.7 constant_dynamic-slice_fusion.2
  520.7 0.7 constant_dynamic-slice_fusion.2
  526.0 0.7 constant_dynamic-slice_fusion.2
  528.6 0.7 constant_dynamic-slice_fusion.2
  536.6 0.7 constant_dynamic-slice_fusion.2
  544.6 0.7 constant_dynamic-slice_fusion.2
  547.2 0.7 constant_dynamic-slice_fusion.2
  552.6 0.7 constant_dynamic-slice_fusion.2
  555.2 0.7 constant_dynamic-slice_fusion.2
  560.5 0.7 constant_dynamic-slice_fusion.2
  563.2 0.7 constant_dynamic-slice_fusion.2
  568.5 0.7 constant_dynamic-slice_fusion.2
  571.2 0.7 constant_dynamic-slice_fusion.2
  576.5 0.7 constant_dynamic-slice_fusion.2
  579.2 0.7 constant_dynamic-slice_fusion.2
  587.1 0.7 constant_dynamic-slice_fusion.2
  595.1 0.7 constant_dynamic-slice_fusion.2
  597.8 0.7 constant_dynamic-slice_fusion.2
  603.1 0.7 constant_dynamic-slice_fusion.2
  605.8 0.7 constant_dynamic-slice_fusion.2
  611.1 0.7 constant_dynamic-slice_fusion.2
  613.7 0.7 constant_dynamic-slice_fusion.2
  619.1 0.7 constant_dynamic-slice_fusion.2
  621.7 0.7 constant_dynamic-slice_fusion.2
  627.0 0.7 constant_dynamic-slice_fusion.2
  629.7 0.7 constant_dynamic-slice_fusion.2
  637.7 0.7 constant_dynamic-slice_fusion.2
  645.6 0.7 constant_dynamic-slice_fusion.2
  648.3 0.7 constant_dynamic-slice_fusion.2
  653.6 0.7 constant_dynamic-slice_fusion.2
  656.3 0.7 constant_dynamic-slice_fusion.2
  661.6 0.7 constant_dynamic-slice_fusion.2
  664.3 0.7 constant_dynamic-slice_fusion.2
  669.6 0.7 constant_dynamic-slice_fusion.2
  672.2 0.7 constant_dynamic-slice_fusion.2
  677.6 0.7 constant_dynamic-slice_fusion.2
  680.2 0.7 constant_dynamic-slice_fusion.2
  688.2 0.7 constant_dynamic-slice_fusion.2
  1145.9 420.4 %while.32 = (s32[]{:T(128)}, f32[256,256]{1,0:T(8,128)S(1)}, f32[256,256]{1,0:T(8,128)S(1)}, s32[]{:T(128)}, s32[]{:T(128)}, /*index=5*/s32[]{:T(128)}, s32[]{:T(128)}) while((s32[]{:T(128)}, f32[256,256]{1,0:T(8,128)S(1)}, f32[256,256]{1,0:T(8,128)S(1)}, s32[]{:T(128)}, s32[]{:T(128)}, /*index=5*/s32[]{:T(128)}, s32[]{:T(128)}) %tuple.83), condition=%wide.region_5.6_spmd.clone, body=%wide.region_4.5_spmd.clone.sunk | while | flops 984328 | bytes 792242 | solution.py:37
  1566.2 3.2 convolution_multiply_fusion
  (3557 shorter events, 864.7 us)
Async XLA Ops:
  7.2 1.2 copy-start
  7.2 16.4 %copy-start.4 = (s32[176,1]{0,1:T(1,128)S(1)}, s32[176,1]{0,1:T(1,128)}, u32[]{:S(2)}) copy-start(s32[176,1]{0,1:T(1,128)} %param.12) | copy-start | bytes 2116
  7.2 16.4 %copy-start.3 = (s32[176,1]{0,1:T(1,128)S(1)}, s32[176,1]{0,1:T(1,128)}, u32[]{:S(2)}) copy-start(s32[176,1]{0,1:T(1,128)} %param.13) | copy-start | bytes 2116
  13.9 118.2 %all-to-all-start = ((bf16[32,2,256,256]{3,2,1,0:T(8,128)(2,1)}), bf16[32,2,256,256]{3,2,1,0:T(8,128)(2,1)}, u32[]{:S(2)}, u32[]{:S(2)}) async-start(bf16[32,2,256,256]{3,2,1,0:T(8,128)(2,1)} %bitcast.57), calls=%async_computation | async-start | bytes 16777216 | tf_op jit(solution)/shard_map/all_to_all | solution.py:49
  23.6 293.4 %reduce-scatter.2.cloned.1.call-start = ((), (), s32[]{:S(2)}) async-start(), calls=%async_computation.2 | async-start | bytes 5242880 | tf_op jit(solution)/shard_map/reduce_scatter | solution.py:58
  183.5 46.6 %copy-start.2 = (s32[176,1]{0,1:T(1,128)S(1)}, s32[176,1]{0,1:T(1,128)}, u32[]{:S(2)}) copy-start(s32[176,1]{0,1:T(1,128)} %param.11) | copy-start | bytes 2116
  230.1 1339.3 %copy-start.1 = (bf16[8,1,256,256]{3,2,1,0:T(8,128)(2,1)S(1)}, bf16[8,1,256,256]{3,2,1,0:T(8,128)(2,1)}, u32[]{:S(2)}) copy-start(bf16[8,1,256,256]{3,2,1,0:T(8,128)(2,1)} %param.15) | copy-start | bytes 3145732
  254.9 209.4 %all-reduce.2.cloned.1.call-start = ((), (), s32[]{:S(2)}) async-start(), calls=%async_computation.3 | async-start | bytes 524288 | tf_op jit(solution)/shard_map/psum | solution.py:60
Sparse Core Ops, SparseCore 0:
  255.0 61.9 reduce-scatter.1
  323.0 141.2 all-reduce.1
where the time goes:
time: 1600 us; the launch traced here: 1580 us
  local copies, waits for them, and re-layouts  577 us (36%)
  waiting for transfers between devices  314 us (20%)
  matrix products  233 us (15%)
  other arithmetic  227 us (14%)
  loops' own time  202 us (13%)
    dynamic_slice x256, local copies, waits for them, and re-layouts, row_fill(): target = lax.dynamic_index_in_dim(gram, j, 0, keepdims=False)  190 us
    another operation x1, loops' own time, upper_factor(): lax.fori_loop(0, width, row_fill, jnp.zeros((width, width), jnp.float32))  189 us
    dynamic_slice x256, local copies, waits for them, and re-layouts, row_step(): pivot = lax.dynamic_index_in_dim(row_now, i, 0, keepdims=False)  164 us
    div x256, other arithmetic, row_step(): (unit - jnp.dot(row_now, inverse, precision=lax.Precision.HIGHEST)) / pivot  163 us
    dynamic_slice x256, local copies, waits for them, and re-layouts, row_fill(): pivot = jnp.sqrt(lax.dynamic_index_in_dim(residue, j, 0, keepdims=False))  150 us
    psum x1, waiting for transfers between devices, local(): summed = lax.psum(gram, ('row', 'col'))  143 us
    all_to_all x1, waiting for transfers between devices, local(): lax.all_to_all(outgoing, 'row', split_axis=0, concat_axis=0, tiled=True)  108 us
    reduce_scatter x1, waiting for transfers between devices, local(): lax.psum_scatter(partial_value, 'col', scatter_dimension=0, tiled=True)  61.9 us
  transfers between devices with their start and end apart: 3, of which 3 were waited for; matrix products, arithmetic and copies ran while one was open for 0% of the time, Pallas kernels for 0%

commit v1 on v0

--- a/solution.py
+++ b/solution.py
@@ -1,9 +1,17 @@
+import functools
 import jax
 import jax.numpy as jnp
 from jax import lax
 from jax.sharding import PartitionSpec as P
 
 BR_DEV = 16
+
+
+def unite_slots_now(u_in, along_axis):
+    return jax.lax.all_gather(u_in, along_axis).sum(axis=0)
+
+
+take_clusters_on_mesh = functools.partial(unite_slots_now, along_axis=("row", "col"))
 
 
 def upper_factor(gram):
@@ -57,7 +65,7 @@
     partial_value = partial_value.reshape(-1, rank_width)
     local_y = lax.psum_scatter(partial_value, "col", scatter_dimension=0, tiled=True)
     gram = jnp.dot(local_y.T, local_y, precision=lax.Precision.HIGHEST)
-    summed = lax.psum(gram, ("row", "col"))
+    summed = take_clusters_on_mesh(gram)
     upper = upper_factor(summed)
     cells_all = local_y.shape[0] * lax.axis_size("row") * lax.axis_size("col")
     scale = jnp.sqrt(jnp.float32(cells_all))

time: 1600 us -> 1390 us (0.87)
  local copies, waits for them, and re-layouts: 577 us -> 408 us
  waiting for transfers between devices: 314 us -> 277 us
    dynamic_slice x256, local copies, waits for them, and re-layouts: 190 us -> 10.5 us  [row_fill(): target = lax.dynamic_index_in_dim(gram, j, 0, keepdims=False)]
    psum x1 -> x0, waiting for transfers between devices: 143 us -> none  [local(): summed = lax.psum(gram, ('row', 'col'))]
    all_gather x0 -> x1, waiting for transfers between devices: none -> 107 us  [unite_slots_now(): return jax.lax.all_gather(u_in, along_axis).sum(axis=0)]
where the time goes in v1:
time: 1390 us; the launch traced here: 1380 us
  local copies, waits for them, and re-layouts  408 us (29%)
  waiting for transfers between devices  277 us (20%)
  other arithmetic  236 us (17%)
  matrix products  232 us (17%)
  loops' own time  205 us (15%)
  between operations  14.2 us (1%)
    another operation x1, loops' own time, upper_factor(): lax.fori_loop(0, width, row_fill, jnp.zeros((width, width), jnp.float32))  193 us
    dynamic_slice x256, local copies, waits for them, and re-layouts, row_step(): pivot = lax.dynamic_index_in_dim(row_now, i, 0, keepdims=False)  174 us
    div x256, other arithmetic, row_step(): (unit - jnp.dot(row_now, inverse, precision=lax.Precision.HIGHEST)) / pivot  160 us
    dynamic_slice x256, local copies, waits for them, and re-layouts, row_fill(): pivot = jnp.sqrt(lax.dynamic_index_in_dim(residue, j, 0, keepdims=False))  151 us
    all_to_all x1, waiting for transfers between devices, local(): lax.all_to_all(outgoing, 'row', split_axis=0, concat_axis=0, tiled=True)  108 us
    all_gather x1, waiting for transfers between devices, unite_slots_now(): return jax.lax.all_gather(u_in, along_axis).sum(axis=0)  107 us
    reduce_scatter x1, waiting for transfers between devices, local(): lax.psum_scatter(partial_value, 'col', scatter_dimension=0, tiled=True)  61.9 us
    dot_general x256, matrix products, row_fill(): residue = target - jnp.dot(known, upper, precision=lax.Precision.HIGHEST)  60.5 us
  transfers between devices with their start and end apart: 3, of which 3 were waited for; matrix products, arithmetic and copies ran while one was open for 0% of the time, Pallas kernels for 0%

profile of v1, /device:TPU:1, one launch (start us, length us, event | category | flops | bytes accessed | tf_op | source)
XLA Modules:
  0.0 1382.2 jit_solution(14344511498001732351)
XLA Ops:
  7.2 0.8 compare_select_fusion.2
  8.4 5.5 gather_fusion
  13.9 9.6 all-to-all-start
  23.7 108.4 %all-to-all-done = bf16[32,2,256,256]{3,2,1,0:T(8,128)(2,1)} async-done(((bf16[32,2,256,256]{3,2,1,0:T(8,128)(2,1)}), bf16[32,2,256,256]{3,2,1,0:T(8,128)(2,1)}, u32[]{:S(2)}, u32[]{:S(2)}) %all-to-all-start) | async-done | bytes 8388640 | tf_op jit(solution)/shard_map/all_to_all | solution.py:57
  132.1 13.8 gather_fusion.1
  145.9 37.6 %fusion.24 = f32[176,256,256]{2,1,0:T(8,128)} fusion(bf16[176,256,256]{2,1,0:T(8,128)(2,1)} %gather_fusion.1, bf16[176,1,256,256]{3,2,1,0:T(8,128)(2,1)} %param.10), kind=kOutput, calls=%fused_computation.32 | convolution fusion | flops 5905580032 | bytes 92274688 | tf_op jit(solution)/shard_map/tij,tjk->tik/dot_general | solution.py:60
  183.5 46.5 %copy.11 = f32[176,256,256]{1,0,2:T(8,128)} copy(f32[176,256,256]{2,1,0:T(8,128)} %fusion.24) | data formatting | bytes 92274688 | tf_op jit(solution)/shard_map/tij,tjk->tik/dot_general | solution.py:60
  230.0 20.3 %fusion.22 = f32[16,256,256]{2,0,1:T(8,128)S(1)} fusion(f32[176,256,256]{1,0,2:T(8,128)} %copy.11, s32[176]{0:T(256)S(1)} %bitcast.65), kind=kOutput, calls=%fused_computation.30 | convolution fusion | flops 2214595328 | bytes 50332352 | tf_op jit(solution)/shard_map/bt,tik->bik/dot_general | solution.py:64
  250.3 4.4 copy.10
  255.0 61.9 %reduce-scatter.2.cloned.1.call-done = f32[1024,256]{1,0:T(8,128)} async-done(((f32[4096,256]{1,0:T(8,128)}), f32[1024,256]{1,0:T(8,128)}) %reduce-scatter.2.cloned.1.call-update) | async-done | bytes 1048592 | tf_op jit(solution)/shard_map/reduce_scatter | solution.py:66
  316.8 4.2 fusion.29
  321.0 107.0 %all-gather.3.cloned.1.call-done = f32[32768,256]{1,0:T(8,128)} async-done(((f32[256,256]{1,0:T(8,128)}), f32[32768,256]{1,0:T(8,128)}) %all-gather.3.cloned.1.call-update) | async-done | bytes 33554448 | tf_op jit(solution)/shard_map/all_gather | solution.py:11
  428.0 12.0 reduce_sum.9
  440.1 505.4 %while.33 = (s32[]{:T(128)}, f32[256,256]{1,0:T(8,128)S(1)}, f32[256,256]{1,0:T(8,128)S(1)}, s32[]{:T(128)}, s32[]{:T(128)}) while((s32[]{:T(128)}, f32[256,256]{1,0:T(8,128)S(1)}, f32[256,256]{1,0:T(8,128)S(1)}, s32[]{:T(128)}, s32[]{:T(128)}) %tuple.80), condition=%wide.region_3.4_spmd.clone.clone, body=%wide.region_2.3_spmd.clone.clone.sunk | while | flops 1902083 | bytes 1063021 | solution.py:30
  945.5 0.7 broadcast_multiply_fusion
  946.2 427.2 %while.32 = (s32[]{:T(128)}, f32[256,256]{1,0:T(8,128)S(1)}, f32[256,256]{1,0:T(8,128)S(1)}, s32[]{:T(128)}, s32[]{:T(128)}, /*index=5*/s32[]{:T(128)}, s32[]{:T(128)}) while((s32[]{:T(128)}, f32[256,256]{1,0:T(8,128)S(1)}, f32[256,256]{1,0:T(8,128)S(1)}, s32[]{:T(128)}, s32[]{:T(128)}, /*index=5*/s32[]{:T(128)}, s32[]{:T(128)}) %tuple.83), condition=%wide.region_5.6_spmd.clone, body=%wide.region_4.5_spmd.clone.sunk | while | flops 984328 | bytes 792242 | solution.py:45
  948.1 0.7 dynamic_slice.50
  949.7 0.7 dynamic_slice.50
  951.4 0.7 dynamic_slice.50
  953.1 0.7 dynamic_slice.50
  954.7 0.7 dynamic_slice.50
  956.4 0.7 dynamic_slice.50
  958.1 0.7 dynamic_slice.50
  959.7 0.7 dynamic_slice.50
  961.4 0.7 dynamic_slice.50
  963.1 0.7 dynamic_slice.50
  964.7 0.7 dynamic_slice.50
  966.4 0.7 dynamic_slice.50
  968.1 0.7 dynamic_slice.50
  969.8 0.7 dynamic_slice.50
  971.4 0.7 dynamic_slice.50
  973.1 0.7 dynamic_slice.50
  974.8 0.7 dynamic_slice.50
  976.4 0.7 dynamic_slice.50
  978.1 0.7 dynamic_slice.50
  979.8 0.7 dynamic_slice.50
  981.4 0.7 dynamic_slice.50
  983.1 0.7 dynamic_slice.50
  984.8 0.7 dynamic_slice.50
  986.4 0.7 dynamic_slice.50
  988.1 0.7 dynamic_slice.50
  989.8 0.7 dynamic_slice.50
  991.4 0.7 dynamic_slice.50
  993.1 0.7 dynamic_slice.50
  994.8 0.7 dynamic_slice.50
  996.5 0.7 dynamic_slice.50
  998.1 0.7 dynamic_slice.50
  999.8 0.7 dynamic_slice.50
  1001.5 0.7 dynamic_slice.50
  1003.1 0.7 dynamic_slice.50
  1004.8 0.7 dynamic_slice.50
  1006.5 0.7 dynamic_slice.50
  1008.1 0.7 dynamic_slice.50
  1009.8 0.7 dynamic_slice.50
  1011.5 0.7 dynamic_slice.50
  1013.1 0.7 dynamic_slice.50
  1014.8 0.7 dynamic_slice.50
  1016.5 0.7 dynamic_slice.50
  1018.2 0.7 dynamic_slice.50
  1019.8 0.7 dynamic_slice.50
  1021.5 0.7 dynamic_slice.50
  1023.2 0.7 dynamic_slice.50
  1024.8 0.7 dynamic_slice.50
  1373.4 2.0 convolution_multiply_fusion
  (3560 shorter events, 696.3 us)
Async XLA Ops:
  7.2 1.2 copy-start
  7.2 16.4 %copy-start.5 = (s32[176,1]{0,1:T(1,128)S(1)}, s32[176,1]{0,1:T(1,128)}, u32[]{:S(2)}) copy-start(s32[176,1]{0,1:T(1,128)} %param.12) | copy-start | bytes 2116
  7.2 16.4 %copy-start.4 = (s32[176,1]{0,1:T(1,128)S(1)}, s32[176,1]{0,1:T(1,128)}, u32[]{:S(2)}) copy-start(s32[176,1]{0,1:T(1,128)} %param.13) | copy-start | bytes 2116
  13.9 118.2 %all-to-all-start = ((bf16[32,2,256,256]{3,2,1,0:T(8,128)(2,1)}), bf16[32,2,256,256]{3,2,1,0:T(8,128)(2,1)}, u32[]{:S(2)}, u32[]{:S(2)}) async-start(bf16[32,2,256,256]{3,2,1,0:T(8,128)(2,1)} %bitcast.58), calls=%async_computation | async-start | bytes 16777216 | tf_op jit(solution)/shard_map/all_to_all | solution.py:57
  23.6 293.2 %reduce-scatter.2.cloned.1.call-start = ((), (), s32[]{:S(2)}) async-start(), calls=%async_computation.2 | async-start | bytes 5242880 | tf_op jit(solution)/shard_map/reduce_scatter | solution.py:66
  183.5 46.5 %copy-start.3 = (s32[176,1]{0,1:T(1,128)S(1)}, s32[176,1]{0,1:T(1,128)}, u32[]{:S(2)}) copy-start(s32[176,1]{0,1:T(1,128)} %param.11) | copy-start | bytes 2116
  254.7 173.3 %all-gather.3.cloned.1.call-start = ((), (), s32[]{:S(2)}) async-start(), calls=%async_computation.3 | async-start | bytes 33816576 | tf_op jit(solution)/shard_map/all_gather | solution.py:11
  316.8 1056.6 %copy-start.2 = (f32[1024,256]{1,0:T(8,128)S(1)}, f32[1024,256]{1,0:T(8,128)}, u32[]{:S(2)}) copy-start(f32[1024,256]{1,0:T(8,128)} %reduce-scatter.2.cloned.1.call-done) | copy-start | bytes 3145732
  428.0 947.4 %copy-start.1 = (bf16[8,1,256,256]{3,2,1,0:T(8,128)(2,1)S(1)}, bf16[8,1,256,256]{3,2,1,0:T(8,128)(2,1)}, u32[]{:S(2)}) copy-start(bf16[8,1,256,256]{3,2,1,0:T(8,128)(2,1)} %param.15) | copy-start | bytes 3145732
Sparse Core Ops, SparseCore 0:
  254.9 61.9 reduce-scatter.1
  321.1 106.8 all-gather.2
